TPU v7x, 32 devices: a whole 2x2x4 slice. The times are simulated.
32 devices in a mesh: dp: 4 (over z), fsdp: 8 (over y, x, core).
Axes of the slice: x: 2, y: 2, z: 4, core: 2. Of those that a mesh axis runs over, the one named last changes fastest.
Arguments:
- hidden: bfloat16 [24576, 8192], P(('dp', 'fsdp')), may hold values from -6 to 6
- head: bfloat16 [512, 8192], P('fsdp'), may hold values from -0.0625 to 0.0625
- labels: int32 [24576], P(('dp', 'fsdp')), may hold values from 0 to 511
- lse: float32 [24576], P(('dp', 'fsdp')), may hold values from 0 to 1.5
- cotangent: float32 [24576], P(('dp', 'fsdp')), may hold values from -0.6 to 0.6
- block_lists: int32 [192, 4], P(('dp', 'fsdp')), may hold values from -1 to 3, as said below
Outputs:
- grad_hidden: bfloat16 [24576, 8192], P(('dp', 'fsdp'))
- grad_head: bfloat16 [512, 8192], P('fsdp', 'dp')
Inputs may be any that keep to these rules, and one draw needn't show every extreme that they name: `block_lists`: each row names distinct vocabulary blocks in its first slots (at least one) and -1 in the remaining slots.
All inputs are finite; a program needn't handle non-finite values.
Results may differ from a plain program's by a relative error of at most 0.0056.
Values may be sent and summed in bfloat16 or wider, within the bound.
A program may use at most 192 MiB of HBM per device.

v0:
```python
import jax
import jax.numpy as jnp
from jax import lax
from jax.sharding import PartitionSpec as P

VB = 128
TB = 128
VBLOCKS = 4


def on_device(hidden, head, labels, lse, cotangent, block_lists):
    blocks_here = block_lists.shape[0]
    vocab = VB * VBLOCKS
    block_ids = jnp.arange(VBLOCKS, dtype=jnp.int32)
    listed = jnp.any(block_lists[:, :, None] == block_ids[None, None, :], axis=1)
    listed_tokens = jnp.repeat(listed, TB, axis=0)
    full_head = lax.all_gather(head, "fsdp", axis=0, tiled=True)
    label_block = labels // VB
    label_listed = jnp.any(
        jnp.logical_and(label_block[:, None] == block_ids[None, :], listed_tokens), axis=1
    )
    extra = jnp.where(label_listed, 0.0, -cotangent).astype(jnp.bfloat16).astype(jnp.float32)
    label_rows = jnp.take(full_head, labels, axis=0)
    grad_acc = extra[:, None] * label_rows.astype(jnp.float32)
    vocab_ids = jnp.arange(vocab, dtype=jnp.int32)
    scaled_hits = jnp.where(vocab_ids[:, None] == labels[None, :], extra[None, :], 0.0).astype(
        jnp.bfloat16
    )
    term_acc = jnp.dot(scaled_hits, hidden, preferred_element_type=jnp.float32)

    def block_pass(block_index, carry):
        grad_all, term_all = carry
        first = block_index * TB
        rows_here = lax.dynamic_slice_in_dim(hidden, first, TB, 0)
        targets = lax.dynamic_slice_in_dim(labels, first, TB, 0)
        norms = lax.dynamic_slice_in_dim(lse, first, TB, 0)
        scales = lax.dynamic_slice_in_dim(cotangent, first, TB, 0)
        grad_rows = lax.dynamic_slice_in_dim(grad_all, first, TB, 0)
        entries = block_lists[block_index]
        count = jnp.sum((entries >= 0).astype(jnp.int32))

        def tile_pass(slot, inner):
            grad_here, term_here = inner
            vocab_block = entries[slot]
            offset = vocab_block * VB
            head_rows = lax.dynamic_slice_in_dim(full_head, offset, VB, 0)
            logits = lax.dot_general(
                rows_here, head_rows, (((1,), (1,)), ((), ())), preferred_element_type=jnp.float32
            )
            columns = offset + jnp.arange(VB, dtype=jnp.int32)
            hits = (targets[:, None] == columns[None, :]).astype(jnp.float32)
            grad_logits = (scales[:, None] * (jnp.exp(logits - norms[:, None]) - hits)).astype(
                jnp.bfloat16
            )
            grad_here = grad_here + jnp.dot(
                grad_logits, head_rows, preferred_element_type=jnp.float32
            )
            update = lax.dot_general(
                grad_logits, rows_here, (((0,), (0,)), ((), ())), preferred_element_type=jnp.float32
            )
            previous = lax.dynamic_slice_in_dim(term_here, offset, VB, 0)
            term_here = lax.dynamic_update_slice_in_dim(term_here, previous + update, offset, 0)
            return (grad_here, term_here)

        grad_rows, term_all = lax.fori_loop(0, count, tile_pass, (grad_rows, term_all))
        grad_all = lax.dynamic_update_slice_in_dim(grad_all, grad_rows, first, 0)
        return (grad_all, term_all)

    grad_acc, term_acc = lax.fori_loop(0, blocks_here, block_pass, (grad_acc, term_acc))
    grad_hidden = grad_acc.astype(jnp.bfloat16)
    slab_part = lax.psum_scatter(term_acc, "fsdp", scatter_dimension=0, tiled=True)
    owned = lax.psum_scatter(slab_part, "dp", scatter_dimension=1, tiled=True)
    return (grad_hidden, owned.astype(jnp.bfloat16))


def solution(mesh):
    return jax.shard_map(
        on_device,
        mesh=mesh,
        in_specs=(
            P(("dp", "fsdp"), None),
            P("fsdp", None),
            P(("dp", "fsdp")),
            P(("dp", "fsdp")),
            P(("dp", "fsdp")),
            P(("dp", "fsdp"), None),
        ),
        out_specs=(P(("dp", "fsdp"), None), P("fsdp", "dp")),
        check_vma=False,
    )
```

profile of v0, /device:TPU:0, one launch (start us, length us, event | category | flops | bytes accessed | tf_op | source)
XLA Modules:
  0.0 718.3 jit_solution(12558813527039458845)
XLA Ops:
  11.7 14.7 %fusion.26 = f32[512,8192]{1,0:T(8,128)} fusion(bf16[768,8192]{1,0:T(8,128)(2,1)} %param.10, f32[768]{0:T(1024)S(1)} %fusion.36, s32[768]{0:T(1024)} %param.12), kind=kOutput, calls=%fused_computation.26 | convolution fusion | flops 6443237376 | bytes 29366272 | tf_op jit(solution)/shard_map/dot_general | solution.py:29
  26.4 40.6 %all-gather.2.cloned.1.call-done = bf16[512,8192]{1,0:T(8,128)(2,1)} async-done(((bf16[64,8192]{1,0:T(8,128)(2,1)}), bf16[512,8192]{1,0:T(8,128)(2,1)}) %all-gather.2.cloned.1.call-update) | async-done | bytes 8388624 | tf_op jit(solution)/shard_map/all_gather | solution.py:17
  67.0 26.5 %gather_fusion = bf16[768,8192]{1,0:T(8,128)(2,1)} fusion(bf16[512,8192]{1,0:T(8,128)(2,1)} %all-gather.2.cloned.1.call-done, s32[1024]{0:T(1024)S(1)} %pad_clamp_fusion), kind=kCustom, calls=%fused_computation | custom fusion | bytes 25168896 | tf_op jit(solution)/shard_map/jit(_take)/gather | solution.py:23
  93.5 14.6 %convert_multiply_fusion = f32[768,8192]{1,0:T(8,128)} fusion(bf16[768,8192]{1,0:T(8,128)(2,1)} %gather_fusion, f32[768]{0:T(1024)S(1)} %fusion.36, pred[768]{0:T(1024)(128)(4,1)S(1)} %compare_and_fusion), kind=kLoop, calls=%fused_computation.23 | loop fusion | flops 18874368 | bytes 37752576 | tf_op jit(solution)/shard_map/mul | solution.py:24
  108.1 425.8 %while.42 = (s32[]{:T(128)}, f32[768,8192]{1,0:T(8,128)}, f32[512,8192]{1,0:T(8,128)}, s32[6,4]{1,0:T(8,128)S(1)}, bf16[768,8192]{1,0:T(8,128)(2,1)}, /*index=5*...) while((s32[]{:T(128)}, f32[768,8192]{1,0:T(8,128)}, ...), condition=%wide.region_6.7_spmd, body=%wide.region_2.0_spmd.sunk | while | flops 807501952 | bytes 46241948 | solution.py:69
  117.4 59.6 %while.43 = (s32[]{:T(128)}, f32[128,8192]{1,0:T(8,128)}, f32[512,8192]{1,0:T(8,128)}, s32[]{:T(128)}, f32[128]{0:T(128)S(1)}, /*index=5*/s32[4]{0:T(128)S(1)}, ...) while((s32[]{:T(128)}, f32[128,8192]{1,0:T(8,128)}, ...), condition=%wide.region_5.5_spmd, body=%wide.region_4.4_spmd.sunk | while | flops 807501952 | bytes 25266944 | solution.py:65
  136.4 5.6 convolution_add_fusion.3
  151.2 5.6 convolution_add_fusion.3
  166.0 5.6 convolution_add_fusion.3
  190.8 44.9 %while.43 = (s32[]{:T(128)}, f32[128,8192]{1,0:T(8,128)}, f32[512,8192]{1,0:T(8,128)}, s32[]{:T(128)}, f32[128]{0:T(128)S(1)}, /*index=5*/s32[4]{0:T(128)S(1)}, ...) while((s32[]{:T(128)}, f32[128,8192]{1,0:T(8,128)}, ...), condition=%wide.region_5.5_spmd, body=%wide.region_4.4_spmd.sunk | while | flops 807501952 | bytes 25266944 | solution.py:65
  195.1 5.6 convolution_add_fusion.3
  209.8 5.6 convolution_add_fusion.3
  224.5 5.6 convolution_add_fusion.3
  249.5 59.6 %while.43 = (s32[]{:T(128)}, f32[128,8192]{1,0:T(8,128)}, f32[512,8192]{1,0:T(8,128)}, s32[]{:T(128)}, f32[128]{0:T(128)S(1)}, /*index=5*/s32[4]{0:T(128)S(1)}, ...) while((s32[]{:T(128)}, f32[128,8192]{1,0:T(8,128)}, ...), condition=%wide.region_5.5_spmd, body=%wide.region_4.4_spmd.sunk | while | flops 807501952 | bytes 25266944 | solution.py:65
  253.8 5.6 convolution_add_fusion.3
  268.5 5.6 convolution_add_fusion.3
  283.2 5.6 convolution_add_fusion.3
  298.1 5.6 convolution_add_fusion.3
  323.0 59.6 %while.43 = (s32[]{:T(128)}, f32[128,8192]{1,0:T(8,128)}, f32[512,8192]{1,0:T(8,128)}, s32[]{:T(128)}, f32[128]{0:T(128)S(1)}, /*index=5*/s32[4]{0:T(128)S(1)}, ...) while((s32[]{:T(128)}, f32[128,8192]{1,0:T(8,128)}, ...), condition=%wide.region_5.5_spmd, body=%wide.region_4.4_spmd.sunk | while | flops 807501952 | bytes 25266944 | solution.py:65
  342.0 5.6 convolution_add_fusion.3
  356.7 5.6 convolution_add_fusion.3
  371.5 5.6 convolution_add_fusion.3
  396.4 59.6 %while.43 = (s32[]{:T(128)}, f32[128,8192]{1,0:T(8,128)}, f32[512,8192]{1,0:T(8,128)}, s32[]{:T(128)}, f32[128]{0:T(128)S(1)}, /*index=5*/s32[4]{0:T(128)S(1)}, ...) while((s32[]{:T(128)}, f32[128,8192]{1,0:T(8,128)}, ...), condition=%wide.region_5.5_spmd, body=%wide.region_4.4_spmd.sunk | while | flops 807501952 | bytes 25266944 | solution.py:65
  430.1 5.6 convolution_add_fusion.3
  445.0 5.6 convolution_add_fusion.3
  469.8 59.6 %while.43 = (s32[]{:T(128)}, f32[128,8192]{1,0:T(8,128)}, f32[512,8192]{1,0:T(8,128)}, s32[]{:T(128)}, f32[128]{0:T(128)S(1)}, /*index=5*/s32[4]{0:T(128)S(1)}, ...) while((s32[]{:T(128)}, f32[128,8192]{1,0:T(8,128)}, ...), condition=%wide.region_5.5_spmd, body=%wide.region_4.4_spmd.sunk | while | flops 807501952 | bytes 25266944 | solution.py:65
  474.1 5.6 convolution_add_fusion.3
  488.9 5.6 convolution_add_fusion.3
  518.3 5.6 convolution_add_fusion.3
  534.0 129.8 %reduce-scatter.3.cloned.1.call-done = f32[64,8192]{1,0:T(8,128)} async-done(((f32[512,8192]{1,0:T(8,128)}), f32[64,8192]{1,0:T(8,128)}) %reduce-scatter.3.cloned.1.call-update) | async-done | bytes 2097168 | tf_op jit(solution)/shard_map/reduce_scatter | solution.py:71
  663.8 13.2 %convert_element_type.35 = bf16[768,8192]{1,0:T(8,128)(2,1)} convert(f32[768,8192]{1,0:T(8,128)} %get-tuple-element.213) | non-fusion elementwise | flops 6291456 | bytes 37748736 | tf_op jit(solution)/shard_map/convert_element_type | solution.py:70
  677.0 32.9 %reduce-scatter.5.cloned.1.call-done = f32[64,2048]{1,0:T(8,128)} async-done(((f32[64,8192]{1,0:T(8,128)}), f32[64,2048]{1,0:T(8,128)}) %reduce-scatter.5.cloned.1.call-update) | async-done | bytes 524304 | tf_op jit(solution)/shard_map/reduce_scatter | solution.py:72
  (154 shorter events, 297.6 us)
Async XLA Ops:
  7.2 59.8 %all-gather.2.cloned.1.call-start = ((), (), s32[]{:S(2)}) async-start(), calls=%async_computation.2 | async-start | bytes 9437184 | tf_op jit(solution)/shard_map/all_gather | solution.py:17
  7.9 655.9 %reduce-scatter.3.cloned.1.call-start = ((), (), s32[]{:S(2)}) async-start(), calls=%async_computation.3 | async-start | bytes 18874368 | tf_op jit(solution)/shard_map/reduce_scatter | solution.py:71
  534.0 176.0 %reduce-scatter.5.cloned.1.call-start = ((), (), s32[]{:S(2)}) async-start(), calls=%async_computation.4 | async-start | bytes 2621440 | tf_op jit(solution)/shard_map/reduce_scatter | solution.py:72
Sparse Core Ops, SparseCore 0:
  9.9 57.0 all-gather.1
  534.1 129.6 reduce-scatter.2
  666.1 43.8 reduce-scatter.4
where the time goes:
time: 723 us; the launch traced here: 718 us
  matrix products  308 us (43%)
  waiting for transfers between devices  204 us (28%)
  local copies, waits for them, and re-layouts  121 us (17%)
  other arithmetic  36.5 us (5%)
  loops' own time  34.2 us (5%)
  between operations  13.7 us (2%)
    reduce_scatter x1, waiting for transfers between devices, on_device(): lax.psum_scatter(term_acc, 'fsdp', scatter_dimension=0, tiled=True)  130 us
    dot_general x23, matrix products, tile_pass(): jnp.dot(grad_logits, head_rows, preferred_element_type=jnp.float32)  128 us
    dot_general x23, matrix products, tile_pass(): lax.dot_general(grad_logits, rows_here, (((0,), (0,)), ((), ())), preferr...  112 us
    dot_general x23, matrix products, tile_pass(): lax.dot_general(rows_here, head_rows, (((1,), (1,)), ((), ())), preferred...  53.2 us
    all_gather x1, waiting for transfers between devices, on_device(): full_head = lax.all_gather(head, 'fsdp', axis=0, tiled=True)  40.6 us
    another operation x6, loops' own time, block_pass(): lax.fori_loop(0, count, tile_pass, (grad_rows, term_all))  34.1 us
    reduce_scatter x1, waiting for transfers between devices, on_device(): owned = lax.psum_scatter(slab_part, 'dp', scatter_dimension=1, tiled=True)  32.9 us
    dynamic_slice x6, local copies, waits for them, and re-layouts, block_pass(): grad_rows = lax.dynamic_slice_in_dim(grad_all, first, TB, 0)  27.7 us
  transfers between devices with their start and end apart: 3, of which 3 were waited for; matrix products, arithmetic and copies ran while one was open for 4% of the time, Pallas kernels for 0%

commit v1 on v0

v1 whole, which is shorter than its diff:
```python
import jax
import jax.numpy as jnp
from jax import lax
from jax.experimental import pallas as pl
from jax.experimental.pallas import tpu as pltpu
from jax.sharding import PartitionSpec as P

VB = 128
VBLOCKS = 4
MESH = pl.DeviceIdType.MESH
F32 = jnp.float32
BF16 = jnp.bfloat16


def listed_of(block_lists):
    ids = jnp.arange(VBLOCKS, dtype=jnp.int32)
    return jnp.any(block_lists[:, :, None] == ids[None, None, :], axis=1)


def plain(hidden, head, labels, lse, cotangent, block_lists):
    tokens = hidden.shape[0]
    full_head = lax.all_gather(head, "fsdp", axis=0, tiled=True)
    vocab = full_head.shape[0]
    keep = jnp.repeat(listed_of(block_lists), tokens // block_lists.shape[0], axis=0)
    keep = jnp.repeat(keep, VB, axis=1)
    logits = lax.dot_general(hidden, full_head, (((1,), (1,)), ((), ())), preferred_element_type=F32)
    hits = (labels[:, None] == jnp.arange(vocab, dtype=jnp.int32)[None, :]).astype(F32)
    soft = jnp.where(keep, jnp.exp(logits - lse[:, None]), 0.0)
    grad_logits = (cotangent[:, None] * (soft - hits)).astype(BF16)
    grad_hidden = jnp.dot(grad_logits, full_head, preferred_element_type=F32).astype(BF16)
    term = lax.dot_general(grad_logits, hidden, (((0,), (0,)), ((), ())), preferred_element_type=F32)
    slab = lax.psum_scatter(term, "fsdp", scatter_dimension=0, tiled=True)
    owned = lax.psum_scatter(slab, "dp", scatter_dimension=1, tiled=True)
    return grad_hidden, owned.astype(BF16)


def kernel(
    hid_hbm, head_hbm, aux, gl_hbm, head_out, out,
    hid, headv, acc, gl, glt, own, tosib, fromsib, part, relay, got, zs, zgot,
    s_hid, s_own, s_out, ag_s, ag_r, sib_s, sib_r, rs_s, rs_r, z_s, z_r,
):
    tokens, width = hid.shape
    rows = head_hbm.shape[0]
    half = width // 2
    quarter = width // 4
    tile = 512
    dp = lax.axis_index("dp")
    f = lax.axis_index("fsdp")
    core, x, y = f % 2, (f // 2) % 2, f // 4
    sib = (dp, f + 1 - 2 * core)
    dev_x = (dp, f + 2 - 4 * x)
    dev_y = (dp, f + 4 - 8 * y)
    zdev = [((dp + r) % 4, f) for r in (1, 2, 3)]

    loads = [
        pltpu.make_async_copy(
            hid_hbm.at[:, pl.ds(i * quarter, quarter)], hid.at[:, pl.ds(i * quarter, quarter)], s_hid.at[i]
        )
        for i in range(4)
    ]
    for c in loads:
        c.start()
    own_copy = pltpu.make_async_copy(head_hbm, headv.at[0], s_own)
    own_copy.start()

    barrier = pltpu.get_barrier_semaphore()
    for d in [sib, dev_x, dev_y] + zdev:
        pl.semaphore_signal(barrier, inc=1, device_id=d, device_id_type=MESH)
    pl.semaphore_wait(barrier, 6)

    sent = []

    def send(src, dst, ssem, rsem, dev):
        c = pltpu.make_async_remote_copy(
            src_ref=src, dst_ref=dst, send_sem=ssem, recv_sem=rsem, device_id=dev, device_id_type=MESH
        )
        c.start()
        sent.append(c)
        return c

    def ag(src, dst, i, dev):
        return send(src, dst, ag_s.at[i], ag_r.at[i], dev)

    lo, hi = pl.ds(0, half), pl.ds(half, half)
    a_x = ag(head_hbm, headv.at[2], 0, dev_x)
    a_y = ag(head_hbm, headv.at[4], 1, dev_y)
    a_sib = ag(head_hbm, headv.at[1], 2, sib)

    def gradients(j):
        acc[...] = jnp.zeros_like(acc)

        @pl.loop(0, width // 1024)
        def _(i):
            cols = pl.ds(pl.multiple_of(i * 1024, 1024), 1024)
            rows_j = headv[2 * j : 2 * j + 2, :, cols].reshape(2 * rows, 1024)
            acc[...] += lax.dot_general(
                hid[:, cols], rows_j, (((1,), (1,)), ((), ())), preferred_element_type=F32
            )

        lse, cot, spot, keep = aux[:, 0:1], aux[:, 1:2], aux[:, 2:3], aux[:, 4 + j : 5 + j]
        ids = lax.broadcasted_iota(jnp.int32, acc.shape, 1) + 2 * rows * j
        hits = jnp.where(ids.astype(F32) == spot, 1.0, 0.0)
        g = cot * (jnp.where(keep > 0.5, jnp.exp(acc[...] - lse), 0.0) - hits)
        gl[:, 2 * rows * j : 2 * rows * (j + 1)] = g.astype(BF16)
        glt[j] = g.T.astype(BF16)

        @pl.loop(0, width // tile)
        def _(i):
            cols = pl.ds(pl.multiple_of(i * tile, tile), tile)
            t = jnp.dot(glt[j], hid[:, cols], preferred_element_type=F32)
            own[j, :, cols] = t[:rows]
            tosib[j, :, cols] = t[rows:].astype(BF16)

        return send(tosib.at[j], fromsib.at[j], sib_s.at[j], sib_r.at[j], sib)

    def pair_sum(j, c):
        c.wait_recv()

        @pl.loop(0, width // tile)
        def _(i):
            cols = pl.ds(pl.multiple_of(i * tile, tile), tile)
            total = own[j, :, cols] + fromsib[j, :, cols].astype(F32)
            if j == 0:
                own[0, :, cols] = total
            else:
                part[j - 1, :, cols] = total.astype(BF16)

    for c in loads:
        c.wait()
    own_copy.wait()
    a_sib.wait_recv()
    c0 = gradients(0)
    a_x.wait_recv()
    r_y = ag(headv.at[2, :, lo], headv.at[6, :, lo], 3, dev_y)
    f_x = ag(headv.at[2], headv.at[3], 4, sib)
    a_y.wait_recv()
    r_x = ag(headv.at[4, :, hi], headv.at[6, :, hi], 5, dev_x)
    f_y = ag(headv.at[4], headv.at[5], 6, sib)
    pair_sum(0, c0)
    f_x.wait_recv()
    c1 = gradients(1)
    pair_sum(1, c1)
    d_x = send(part.at[0, :, lo], got.at[0, :, lo], rs_s.at[0], rs_r.at[0], dev_x)
    r_y.wait_recv()
    f_lo = ag(headv.at[6, :, lo], headv.at[7, :, lo], 7, sib)
    r_x.wait_recv()
    f_hi = ag(headv.at[6, :, hi], headv.at[7, :, hi], 8, sib)
    f_y.wait_recv()
    c2 = gradients(2)
    pair_sum(2, c2)
    d_y = send(part.at[1, :, hi], got.at[1, :, hi], rs_s.at[1], rs_r.at[1], dev_y)
    f_lo.wait_recv()
    f_hi.wait_recv()
    c3 = gradients(3)
    keep_head = pltpu.make_async_copy(headv, head_out, s_out.at[0])
    keep_head.start()
    keep_gl = pltpu.make_async_copy(gl, gl_hbm, s_out.at[1])
    keep_gl.start()
    pair_sum(3, c3)
    v_x = send(part.at[2, :, lo], relay.at[:, lo], rs_s.at[2], rs_r.at[2], dev_x)
    v_y = send(part.at[2, :, hi], relay.at[:, hi], rs_s.at[3], rs_r.at[3], dev_y)

    def joined(c, p, first):
        c.wait_recv()

        @pl.loop(0, half // tile)
        def _(i):
            cols = pl.ds(pl.multiple_of(first + i * tile, tile), tile)
            part[p, :, cols] = (part[p, :, cols].astype(F32) + relay[:, cols].astype(F32)).astype(BF16)

    joined(v_x, 1, 0)
    e_y = send(part.at[1, :, lo], got.at[1, :, lo], rs_s.at[4], rs_r.at[4], dev_y)
    joined(v_y, 0, half)
    e_x = send(part.at[0, :, hi], got.at[0, :, hi], rs_s.at[5], rs_r.at[5], dev_x)
    for c in (d_x, d_y, e_y, e_x):
        c.wait_recv()

    def slab_sum(first, i):
        cols = pl.ds(pl.multiple_of(first + i * tile, tile), tile)
        return own[0, :, cols] + got[0, :, cols].astype(F32) + got[1, :, cols].astype(F32)

    zc = []
    for r in (2, 1, 3):

        @pl.loop(0, quarter // tile)
        def _(i):
            zs[r - 1, :, pl.ds(pl.multiple_of(i * tile, tile), tile)] = slab_sum(
                ((dp + r) % 4) * quarter, i
            ).astype(BF16)

        zc.append(send(zs.at[r - 1], zgot.at[r - 1], z_s.at[r - 1], z_r.at[r - 1], zdev[r - 1]))
    for c in zc:
        c.wait_recv()

    @pl.loop(0, quarter // tile)
    def _(i):
        cols = pl.ds(pl.multiple_of(i * tile, tile), tile)
        total = slab_sum(dp * quarter, i)
        for r in range(3):
            total = total + zgot[r, :, cols].astype(F32)
        out[:, cols] = total.astype(BF16)

    for c in sent:
        c.wait_send()
    keep_head.wait()
    keep_gl.wait()


def fused(hidden, head, labels, lse, cotangent, block_lists):
    tokens, width = hidden.shape
    rows = head.shape[0]
    f = lax.axis_index("fsdp")
    listed = listed_of(block_lists).astype(F32)
    order = jnp.arange(VBLOCKS, dtype=jnp.int32) ^ (f // 2)
    mine = jnp.sum(
        jnp.where(order[None, :, None] == jnp.arange(VBLOCKS)[None, None, :], listed[:, None, :], 0.0), axis=2
    )
    keep = jnp.repeat(mine, tokens // block_lists.shape[0], axis=0)
    spot = ((labels // rows) ^ f) * rows + labels % rows
    aux = jnp.concatenate(
        [lse[:, None], cotangent[:, None], spot.astype(F32)[:, None], jnp.zeros((tokens, 1), F32), keep,
         jnp.zeros((tokens, 120), F32)], axis=1,
    )
    vm = pltpu.VMEM
    dma = pltpu.SemaphoreType.DMA
    any_ = pl.BlockSpec(memory_space=pl.ANY)
    vmem = pl.BlockSpec(memory_space=pltpu.VMEM)
    gl, full, owned = pl.pallas_call(
        kernel,
        out_shape=(
            jax.ShapeDtypeStruct((tokens, 8 * rows), BF16),
            jax.ShapeDtypeStruct((8, rows, width), BF16),
            jax.ShapeDtypeStruct((rows, width // 4), BF16),
        ),
        in_specs=[any_, any_, vmem],
        out_specs=(any_, any_, vmem),
        scratch_shapes=[
            vm((tokens, width), BF16), vm((8, rows, width), BF16), vm((tokens, 2 * rows), F32),
            vm((tokens, 8 * rows), BF16), vm((4, 2 * rows, tokens), BF16),
            vm((4, rows, width), F32), vm((4, rows, width), BF16), vm((4, rows, width), BF16),
            vm((3, rows, width), BF16), vm((rows, width), BF16), vm((2, rows, width), BF16),
            vm((3, rows, width // 4), BF16), vm((3, rows, width // 4), BF16),
            dma((4,)), dma, dma((2,)), dma((9,)), dma((9,)), dma((4,)), dma((4,)),
            dma((6,)), dma((6,)), dma((3,)), dma((3,)),
        ],
        compiler_params=pltpu.CompilerParams(
            collective_id=0, has_side_effects=True, vmem_limit_bytes=58 * 1024 * 1024
        ),
    )(hidden, head, aux)
    grad_hidden = jnp.dot(gl, full.reshape(8 * rows, width), preferred_element_type=F32).astype(BF16)
    return grad_hidden, owned


def solution(mesh):
    small = mesh.shape["dp"] == 4 and mesh.shape["fsdp"] == 8
    return jax.shard_map(
        fused if small else plain,
        mesh=mesh,
        in_specs=(
            P(("dp", "fsdp"), None),
            P("fsdp", None),
            P(("dp", "fsdp")),
            P(("dp", "fsdp")),
            P(("dp", "fsdp")),
            P(("dp", "fsdp"), None),
        ),
        out_specs=(P(("dp", "fsdp"), None), P("fsdp", "dp")),
        check_vma=False,
    )
```

time: 723 us -> 135 us (0.19)
  matrix products: 308 us -> 13.1 us
  waiting for transfers between devices: 204 us -> 0 us
  local copies, waits for them, and re-layouts: 121 us -> 4.24 us
  Pallas kernels: 0 us -> 113 us
  other arithmetic: 36.5 us -> 1.57 us
  loops' own time: 34.2 us -> 0 us
  between operations: 13.7 us -> 0.72 us
    dot_general x70 -> x1, matrix products: 308 us -> 13.1 us  [fused(): jnp.dot(gl, full.reshape(8 * rows, width), preferred_element_type=F32)]
    reduce_scatter x2 -> x0, waiting for transfers between devices: 163 us -> none  [the longest x1 130 us: on_device(): lax.psum_scatter(term_acc, 'fsdp', scatter_dimension=0, tiled=True)]
    pallas_call x0 -> x1, Pallas kernels: none -> 113 us  [fused(): pl.pallas_call(kernel, out_shape=(jax.ShapeDtypeStruct((tokens, 8 * rows)...]
    dynamic_slice x53 -> x0, local copies, waits for them, and re-layouts: 66.7 us -> none  [the longest x6 27.7 us: block_pass(): grad_rows = lax.dynamic_slice_in_dim(grad_all, first, TB, 0)]
    all_gather x1 -> x0, waiting for transfers between devices: 40.6 us -> none  [on_device(): full_head = lax.all_gather(head, 'fsdp', axis=0, tiled=True)]
    another operation x7 -> x0, loops' own time: 34.2 us -> none  [the longest x6 34.1 us: block_pass(): lax.fori_loop(0, count, tile_pass, (grad_rows, term_all))]
    dynamic_update_slice x6 -> x0, local copies, waits for them, and re-layouts: 27.3 us -> none  [block_pass(): grad_all = lax.dynamic_update_slice_in_dim(grad_all, grad_rows, first, 0)]
    gather x1 -> x0, local copies, waits for them, and re-layouts: 26.5 us -> none  [on_device(): label_rows = jnp.take(full_head, labels, axis=0)]
  transfers between devices with their start and end apart: 3 -> 0, of which waited for: 3 -> 0; matrix products, arithmetic and copies ran while one was open for 4% -> 0% of each run, Pallas kernels for 0% -> 0%
where the time goes in v1:
time: 135 us; the launch traced here: 132 us
  Pallas kernels  113 us (84%)
  matrix products  13.1 us (10%)
  local copies, waits for them, and re-layouts  4.24 us (3%)
  other arithmetic  1.57 us (1%)
    pallas_call x1, Pallas kernels, fused(): pl.pallas_call(kernel, out_shape=(jax.ShapeDtypeStruct((tokens, 8 * rows)...  113 us
    dot_general x1, matrix products, fused(): jnp.dot(gl, full.reshape(8 * rows, width), preferred_element_type=F32)  13.1 us

profile of v1, /device:TPU:0, one launch (start us, length us, event | category | flops | bytes accessed | tf_op | source)
XLA Modules:
  0.0 132.3 jit_solution(14416860080948787317)
XLA Ops:
  0.7 0.1 iota_compare_fusion.1
  0.7 0.7 fusion
  1.4 0.1 select_reduce_fusion
  1.5 0.1 copy.13
  1.6 0.7 fusion.4
  2.3 0.2 broadcast_in_dim.54
  2.5 0.8 broadcast_in_dim.52
  3.4 0.8 broadcast_in_dim.53
  4.3 1.5 %concatenate.3.aux = f32[768,128]{1,0:T(8,128)} concatenate(f32[768,1]{1,0:T(8,128)S(1)} %broadcast_in_dim.52, f32[768,1]{1,0:T(8,128)S(1)} %broadcast_in_dim.53, f32[768,1]{1,0:T(8,128)S(1)} %broadcast_in_dim.54, f32[768,1]{1,0:T(8,128)S(1)} %broadcast_in_dim.46, f32[768,4]{1,0:T(8,128)S(1)} %bitcast.4, f32[768,120]{1,0:T(8,128)S(1)} %broadcast_in_dim.51), dimensions={1} | concatenate | bytes 786432 | tf_op jit(solution)/shard_map/concatenate | solution.py:220
  5.8 112.6 %shard_map.77 = (bf16[768,512]{1,0:T(8,128)(2,1)}, bf16[8,64,8192]{2,1,0:T(8,128)(2,1)}, bf16[64,2048]{1,0:T(8,128)(2,1)}) custom-call(bf16[768,8192]{1,0:T(8,128)(2,1)} %hid_hbm.1, bf16[64,8192]{1,0:T(8,128)(2,1)} %head_hbm.1, f32[768,128]{1,0:T(8,128)} %concatenate.3.aux), custom_call_target="tpu_custom_call" | custom-call | tf_op jit(solution)/shard_map/pallas_call | solution.py:228
  118.4 0.0 copy-start
  118.4 13.1 %convolution_convert_fusion = bf16[768,8192]{1,0:T(8,128)(2,1)} fusion(bf16[768,512]{1,0:T(8,128)(2,1)} %get-tuple-element.5, bf16[512,8192]{1,0:T(8,128)(2,1)} %bitcast.5), kind=kOutput, calls=%fused_computation | convolution fusion | flops 6448742400 | bytes 21757952 | tf_op jit(solution)/shard_map/dot_general | solution.py:250
  131.6 0.0 copy-done
  131.6 0.7 copy.18
  (5 shorter events, 0.1 us)
Async XLA Ops:
  118.4 13.2 %copy-start = (bf16[64,2048]{1,0:T(8,128)(2,1)S(1)}, bf16[64,2048]{1,0:T(8,128)(2,1)}, u32[]{:S(2)}) copy-start(bf16[64,2048]{1,0:T(8,128)(2,1)} %get-tuple-element.11) | copy-start | bytes 786436

commit v2 on v1

--- a/solution.py
+++ b/solution.py
@@ -86,7 +86,13 @@
     a_y = ag(head_hbm, headv.at[4], 1, dev_y)
     a_sib = ag(head_hbm, headv.at[1], 2, sib)
 
-    def gradients(j):
+    def cols_at(first, i):
+        return pl.ds(pl.multiple_of(first + i * tile, tile), tile)
+
+    def piece(p):
+        return pl.ds(p * quarter, quarter)
+
+    def logits_grad(j):
         acc[...] = jnp.zeros_like(acc)
 
         @pl.loop(0, width // 1024)
@@ -94,36 +100,43 @@
             cols = pl.ds(pl.multiple_of(i * 1024, 1024), 1024)
             rows_j = headv[2 * j : 2 * j + 2, :, cols].reshape(2 * rows, 1024)
             acc[...] += lax.dot_general(
-                hid[:, cols], rows_j, (((1,), (1,)), ((), ())), preferred_element_type=F32
+                rows_j, hid[:, cols], (((1,), (1,)), ((), ())), preferred_element_type=F32
             )
 
-        lse, cot, spot, keep = aux[:, 0:1], aux[:, 1:2], aux[:, 2:3], aux[:, 4 + j : 5 + j]
-        ids = lax.broadcasted_iota(jnp.int32, acc.shape, 1) + 2 * rows * j
+        lse, cot, spot, keep = aux[0:1, :], aux[1:2, :], aux[2:3, :], aux[4 + j : 5 + j, :]
+        ids = lax.broadcasted_iota(jnp.int32, acc.shape, 0) + 2 * rows * j
         hits = jnp.where(ids.astype(F32) == spot, 1.0, 0.0)
         g = cot * (jnp.where(keep > 0.5, jnp.exp(acc[...] - lse), 0.0) - hits)
-        gl[:, 2 * rows * j : 2 * rows * (j + 1)] = g.astype(BF16)
-        glt[j] = g.T.astype(BF16)
-
-        @pl.loop(0, width // tile)
+        glt[j] = g.astype(BF16)
+        gl[:, 2 * rows * j : 2 * rows * (j + 1)] = g.T.astype(BF16)
+
+    def terms(j, p):
+        @pl.loop(0, quarter // tile)
         def _(i):
-            cols = pl.ds(pl.multiple_of(i * tile, tile), tile)
-            t = jnp.dot(glt[j], hid[:, cols], preferred_element_type=F32)
+            t = jnp.dot(glt[j], hid[:, cols_at(p * tile, i * 4)], preferred_element_type=F32)
+            cols = cols_at(p * quarter, i)
             own[j, :, cols] = t[:rows]
             tosib[j, :, cols] = t[rows:].astype(BF16)
 
+    def gradients(j):
+        logits_grad(j)
+        for p in range(4):
+            terms(j, p)
         return send(tosib.at[j], fromsib.at[j], sib_s.at[j], sib_r.at[j], sib)
 
-    def pair_sum(j, c):
-        c.wait_recv()
-
-        @pl.loop(0, width // tile)
+    def add_pair(j, first, count):
+        @pl.loop(0, count)
         def _(i):
-            cols = pl.ds(pl.multiple_of(i * tile, tile), tile)
+            cols = cols_at(first, i)
             total = own[j, :, cols] + fromsib[j, :, cols].astype(F32)
             if j == 0:
                 own[0, :, cols] = total
             else:
                 part[j - 1, :, cols] = total.astype(BF16)
+
+    def pair_sum(j, c):
+        c.wait_recv()
+        add_pair(j, 0, width // tile)
 
     for c in loads:
         c.wait()
@@ -151,59 +164,78 @@
     d_y = send(part.at[1, :, hi], got.at[1, :, hi], rs_s.at[1], rs_r.at[1], dev_y)
     f_lo.wait_recv()
     f_hi.wait_recv()
-    c3 = gradients(3)
+    logits_grad(3)
     keep_head = pltpu.make_async_copy(headv, head_out, s_out.at[0])
     keep_head.start()
     keep_gl = pltpu.make_async_copy(gl, gl_hbm, s_out.at[1])
     keep_gl.start()
-    pair_sum(3, c3)
-    v_x = send(part.at[2, :, lo], relay.at[:, lo], rs_s.at[2], rs_r.at[2], dev_x)
-    v_y = send(part.at[2, :, hi], relay.at[:, hi], rs_s.at[3], rs_r.at[3], dev_y)
-
-    def joined(c, p, first):
-        c.wait_recv()
-
-        @pl.loop(0, half // tile)
-        def _(i):
-            cols = pl.ds(pl.multiple_of(first + i * tile, tile), tile)
-            part[p, :, cols] = (part[p, :, cols].astype(F32) + relay[:, cols].astype(F32)).astype(BF16)
-
-    joined(v_x, 1, 0)
-    e_y = send(part.at[1, :, lo], got.at[1, :, lo], rs_s.at[4], rs_r.at[4], dev_y)
-    joined(v_y, 0, half)
-    e_x = send(part.at[0, :, hi], got.at[0, :, hi], rs_s.at[5], rs_r.at[5], dev_x)
-    for c in (d_x, d_y, e_y, e_x):
-        c.wait_recv()
-
-    def slab_sum(first, i):
-        cols = pl.ds(pl.multiple_of(first + i * tile, tile), tile)
-        return own[0, :, cols] + got[0, :, cols].astype(F32) + got[1, :, cols].astype(F32)
-
-    zc = []
-    for r in (2, 1, 3):
+    order = (0, 2, 1, 3)
+    cs, vs, es = {}, {}, {}
+
+    def pass_on(p):
+        cs[p].wait_recv()
+        add_pair(3, p * quarter, quarter // tile)
+        vs[p] = send(
+            part.at[2, :, piece(p)], relay.at[:, piece(p)], rs_s.at[2 + p], rs_r.at[2 + p], dev_x if p < 2 else dev_y
+        )
+
+    for i in range(4):
+        p = order[i]
+        terms(3, p)
+        cs[p] = send(
+            tosib.at[3, :, piece(p)], fromsib.at[3, :, piece(p)], sib_s.at[3 + p], sib_r.at[3 + p], sib
+        )
+        if i > 0:
+            pass_on(order[i - 1])
+    pass_on(order[3])
+
+    for p in order:
+        vs[p].wait_recv()
+        k = 1 if p < 2 else 0
 
         @pl.loop(0, quarter // tile)
         def _(i):
-            zs[r - 1, :, pl.ds(pl.multiple_of(i * tile, tile), tile)] = slab_sum(
-                ((dp + r) % 4) * quarter, i
-            ).astype(BF16)
-
-        zc.append(send(zs.at[r - 1], zgot.at[r - 1], z_s.at[r - 1], z_r.at[r - 1], zdev[r - 1]))
-    for c in zc:
-        c.wait_recv()
-
-    @pl.loop(0, quarter // tile)
-    def _(i):
-        cols = pl.ds(pl.multiple_of(i * tile, tile), tile)
-        total = slab_sum(dp * quarter, i)
-        for r in range(3):
-            total = total + zgot[r, :, cols].astype(F32)
-        out[:, cols] = total.astype(BF16)
+            cols = cols_at(p * quarter, i)
+            part[k, :, cols] = (part[k, :, cols].astype(F32) + relay[:, cols].astype(F32)).astype(BF16)
+
+        es[p] = send(
+            part.at[k, :, piece(p)], got.at[k, :, piece(p)], rs_s.at[6 + p], rs_r.at[6 + p], dev_y if p < 2 else dev_x
+        )
+
+    def slab_sum(p, q):
+        cols = cols_at(p * quarter, q)
+        return own[0, :, cols] + got[0, :, cols].astype(F32) + got[1, :, cols].astype(F32)
+
+    zc = {}
+    for p in order:
+        if p == order[0]:
+            d_x.wait_recv()
+        if p == order[1]:
+            d_y.wait_recv()
+        es[p].wait_recv()
+        here = pl.ds(p * tile, tile)
+        for r in (2, 1, 3):
+            zs[r - 1, :, here] = slab_sum(p, (dp + r) % 4).astype(BF16)
+            n = 3 * p + r - 1
+            zc[p, r] = send(
+                zs.at[r - 1, :, here], zgot.at[r - 1, :, here], z_s.at[n], z_r.at[n], zdev[r - 1]
+            )
+    for p in order:
+        here = pl.ds(p * tile, tile)
+        total = slab_sum(p, dp)
+        for r in (1, 2, 3):
+            zc[p, r].wait_recv()
+            total = total + zgot[r - 1, :, here].astype(F32)
+        out[:, here] = total.astype(BF16)
 
     for c in sent:
         c.wait_send()
     keep_head.wait()
     keep_gl.wait()
+
+
+def rows_kernel(gl, head, out):
+    out[...] = jnp.dot(gl[...], head[...], preferred_element_type=F32).astype(BF16)
 
 
 def fused(hidden, head, labels, lse, cotangent, block_lists):
@@ -213,13 +245,12 @@
     listed = listed_of(block_lists).astype(F32)
     order = jnp.arange(VBLOCKS, dtype=jnp.int32) ^ (f // 2)
     mine = jnp.sum(
-        jnp.where(order[None, :, None] == jnp.arange(VBLOCKS)[None, None, :], listed[:, None, :], 0.0), axis=2
+        jnp.where(order[:, None, None] == jnp.arange(VBLOCKS)[None, None, :], listed[None, :, :], 0.0), axis=2
     )
-    keep = jnp.repeat(mine, tokens // block_lists.shape[0], axis=0)
+    keep = jnp.repeat(mine, tokens // block_lists.shape[0], axis=1)
     spot = ((labels // rows) ^ f) * rows + labels % rows
     aux = jnp.concatenate(
-        [lse[:, None], cotangent[:, None], spot.astype(F32)[:, None], jnp.zeros((tokens, 1), F32), keep,
-         jnp.zeros((tokens, 120), F32)], axis=1,
+        [lse[None], cotangent[None], spot.astype(F32)[None], jnp.zeros((1, tokens), F32), keep], axis=0
     )
     vm = pltpu.VMEM
     dma = pltpu.SemaphoreType.DMA
@@ -235,19 +266,30 @@
         in_specs=[any_, any_, vmem],
         out_specs=(any_, any_, vmem),
         scratch_shapes=[
-            vm((tokens, width), BF16), vm((8, rows, width), BF16), vm((tokens, 2 * rows), F32),
+            vm((tokens, width), BF16), vm((8, rows, width), BF16), vm((2 * rows, tokens), F32),
             vm((tokens, 8 * rows), BF16), vm((4, 2 * rows, tokens), BF16),
             vm((4, rows, width), F32), vm((4, rows, width), BF16), vm((4, rows, width), BF16),
             vm((3, rows, width), BF16), vm((rows, width), BF16), vm((2, rows, width), BF16),
             vm((3, rows, width // 4), BF16), vm((3, rows, width // 4), BF16),
-            dma((4,)), dma, dma((2,)), dma((9,)), dma((9,)), dma((4,)), dma((4,)),
-            dma((6,)), dma((6,)), dma((3,)), dma((3,)),
+            dma((4,)), dma, dma((2,)), dma((9,)), dma((9,)), dma((7,)), dma((7,)),
+            dma((10,)), dma((10,)), dma((12,)), dma((12,)),
         ],
         compiler_params=pltpu.CompilerParams(
             collective_id=0, has_side_effects=True, vmem_limit_bytes=58 * 1024 * 1024
         ),
     )(hidden, head, aux)
-    grad_hidden = jnp.dot(gl, full.reshape(8 * rows, width), preferred_element_type=F32).astype(BF16)
+    wide = 1024
+    grad_hidden = pl.pallas_call(
+        rows_kernel,
+        out_shape=jax.ShapeDtypeStruct((tokens, width), BF16),
+        grid=(width // wide,),
+        in_specs=[
+            pl.BlockSpec((tokens, 8 * rows), lambda i: (0, 0)),
+            pl.BlockSpec((8 * rows, wide), lambda i: (0, i)),
+        ],
+        out_specs=pl.BlockSpec((tokens, wide), lambda i: (0, i)),
+        compiler_params=pltpu.CompilerParams(vmem_limit_bytes=60 * 1024 * 1024),
+    )(gl, full.reshape(8 * rows, width))
     return grad_hidden, owned
 
 

time: 135 us -> 130 us (0.963); the launches traced: 132 us -> 129 us
  matrix products: 13.1 us -> 0 us
  Pallas kernels: 113 us -> 124 us
  local copies, waits for them, and re-layouts: 4.24 us -> 2.81 us
    pallas_call x0 -> x1, Pallas kernels: none -> 13.2 us  [fused(): pl.pallas_call(rows_kernel, out_shape=jax.ShapeDtypeStruct((tokens, width...]
    dot_general x1 -> x0, matrix products: 13.1 us -> none  [fused(): jnp.dot(gl, full.reshape(8 * rows, width), preferred_element_type=F32)]
    pallas_call x1, Pallas kernels: 113 us -> 111 us  [fused(): pl.pallas_call(kernel, out_shape=(jax.ShapeDtypeStruct((tokens, 8 * rows)...]
where the time goes in v2:
time: 130 us; the launch traced here: 129 us
  Pallas kernels  124 us (95%)
  local copies, waits for them, and re-layouts  2.81 us (2%)
  other arithmetic  1.57 us (1%)
    pallas_call x1, Pallas kernels, fused(): pl.pallas_call(kernel, out_shape=(jax.ShapeDtypeStruct((tokens, 8 * rows)...  111 us
    pallas_call x1, Pallas kernels, fused(): pl.pallas_call(rows_kernel, out_shape=jax.ShapeDtypeStruct((tokens, width...  13.2 us

profile of v2, /device:TPU:0, one launch (start us, length us, event | category | flops | bytes accessed | tf_op | source)
XLA Modules:
  0.0 128.8 jit_solution(16019079857299484735)
XLA Ops:
  0.7 0.1 iota_compare_fusion.1
  0.7 0.7 fusion
  1.4 0.1 select_reduce_fusion
  1.5 0.7 broadcast_in_dim.40
  2.2 0.7 broadcast_in_dim.41
  2.9 0.7 fusion.4
  3.6 0.1 broadcast_bitcast_fusion
  3.7 0.6 concatenate.3.aux
  4.3 110.5 %shard_map.77 = (bf16[768,512]{1,0:T(8,128)(2,1)}, bf16[8,64,8192]{2,1,0:T(8,128)(2,1)}, bf16[64,2048]{1,0:T(8,128)(2,1)}) custom-call(bf16[768,8192]{1,0:T(8,128)(2,1)} %hid_hbm.1, bf16[64,8192]{1,0:T(8,128)(2,1)} %head_hbm.1, f32[8,768]{1,0:T(8,128)} %concatenate.3.aux), custom_call_target="tpu_custom_call" | custom-call | tf_op jit(solution)/shard_map/pallas_call | solution.py:259
  114.8 0.0 copy-start
  114.9 13.2 %shard_map.78 = bf16[768,8192]{1,0:T(8,128)(2,1)} custom-call(bf16[768,512]{1,0:T(8,128)(2,1)} %get-tuple-element.5.gl, bf16[512,8192]{1,0:T(8,128)(2,1)} %bitcast.6), custom_call_target="tpu_custom_call" | custom-call | tf_op jit(solution)/shard_map/pallas_call | solution.py:282
  128.1 0.0 copy-done
  128.1 0.7 copy.14
  (5 shorter events, 0.0 us)
Async XLA Ops:
  114.8 13.2 %copy-start = (bf16[64,2048]{1,0:T(8,128)(2,1)S(1)}, bf16[64,2048]{1,0:T(8,128)(2,1)}, u32[]{:S(2)}) copy-start(bf16[64,2048]{1,0:T(8,128)(2,1)} %get-tuple-element.11) | copy-start | bytes 786436

commit v3 on v2

--- a/solution.py
+++ b/solution.py
@@ -154,12 +154,12 @@
     c1 = gradients(1)
     pair_sum(1, c1)
     d_x = send(part.at[0, :, lo], got.at[0, :, lo], rs_s.at[0], rs_r.at[0], dev_x)
+    f_y.wait_recv()
+    c2 = gradients(2)
     r_y.wait_recv()
     f_lo = ag(headv.at[6, :, lo], headv.at[7, :, lo], 7, sib)
     r_x.wait_recv()
     f_hi = ag(headv.at[6, :, hi], headv.at[7, :, hi], 8, sib)
-    f_y.wait_recv()
-    c2 = gradients(2)
     pair_sum(2, c2)
     d_y = send(part.at[1, :, hi], got.at[1, :, hi], rs_s.at[1], rs_r.at[1], dev_y)
     f_lo.wait_recv()

time: 130 us -> 131 us (level)
    pallas_call x1, Pallas kernels: 111 us -> 112 us  [fused(): pl.pallas_call(kernel, out_shape=(jax.ShapeDtypeStruct((tokens, 8 * rows)...]
where the time goes in v3:
time: 131 us; the launch traced here: 130 us
  Pallas kernels  125 us (95%)
  local copies, waits for them, and re-layouts  2.81 us (2%)
  other arithmetic  1.57 us (1%)
    pallas_call x1, Pallas kernels, fused(): pl.pallas_call(kernel, out_shape=(jax.ShapeDtypeStruct((tokens, 8 * rows)...  112 us
    pallas_call x1, Pallas kernels, fused(): pl.pallas_call(rows_kernel, out_shape=jax.ShapeDtypeStruct((tokens, width...  13.2 us

profile of v3, /device:TPU:0, one launch (start us, length us, event | category | flops | bytes accessed | tf_op | source)
XLA Modules:
  0.0 130.5 jit_solution(5570827948581681417)
XLA Ops:
  0.7 0.1 iota_compare_fusion.1
  0.7 0.7 fusion
  1.4 0.1 select_reduce_fusion
  1.5 0.7 broadcast_in_dim.40
  2.2 0.7 broadcast_in_dim.41
  2.9 0.7 fusion.4
  3.6 0.1 broadcast_bitcast_fusion
  3.7 0.6 concatenate.3.aux
  4.3 112.2 %shard_map.77 = (bf16[768,512]{1,0:T(8,128)(2,1)}, bf16[8,64,8192]{2,1,0:T(8,128)(2,1)}, bf16[64,2048]{1,0:T(8,128)(2,1)}) custom-call(bf16[768,8192]{1,0:T(8,128)(2,1)} %hid_hbm.1, bf16[64,8192]{1,0:T(8,128)(2,1)} %head_hbm.1, f32[8,768]{1,0:T(8,128)} %concatenate.3.aux), custom_call_target="tpu_custom_call" | custom-call | tf_op jit(solution)/shard_map/pallas_call | solution.py:259
  116.5 0.0 copy-start
  116.5 13.2 %shard_map.78 = bf16[768,8192]{1,0:T(8,128)(2,1)} custom-call(bf16[768,512]{1,0:T(8,128)(2,1)} %get-tuple-element.5.gl, bf16[512,8192]{1,0:T(8,128)(2,1)} %bitcast.6), custom_call_target="tpu_custom_call" | custom-call | tf_op jit(solution)/shard_map/pallas_call | solution.py:282
  129.7 0.0 copy-done
  129.7 0.7 copy.14
  (5 shorter events, 0.0 us)
Async XLA Ops:
  116.5 13.2 %copy-start = (bf16[64,2048]{1,0:T(8,128)(2,1)S(1)}, bf16[64,2048]{1,0:T(8,128)(2,1)}, u32[]{:S(2)}) copy-start(bf16[64,2048]{1,0:T(8,128)(2,1)} %get-tuple-element.11) | copy-start | bytes 786436
